TPU v7x, 32 devices: a whole 2x2x4 slice. The times are simulated.
32 devices in a mesh: firm: 8 (over z, y), tm: 4 (over x, core).
Axes of the slice: x: 2, y: 2, z: 4, core: 2. Of those that a mesh axis runs over, the one named last changes fastest.
Arguments:
- features: bfloat16 [4096, 8, 128], P('firm', 'tm'), may hold values from -6 to 6
- cotangent: bfloat16 [4096, 8, 128], P('firm', 'tm'), may hold values from -6 to 6
- tiles: bfloat16 [32, 32, 128, 128], P('firm'), may hold values from -0.1875 to 0.1875
- mask: int32 [32, 32], P('firm'), may hold values 0 or 1
- w_prev: bfloat16 [2, 128, 256], replicated, may hold values from -0.375 to 0.375
- w_cur: bfloat16 [2, 128, 256], replicated, may hold values from -0.375 to 0.375
- w_self: bfloat16 [2, 128, 128], replicated, may hold values from -0.5 to 0.5
- w_nbr: bfloat16 [2, 128, 128], replicated, may hold values from -0.5 to 0.5
- dilations: int32 [2], replicated, may hold values from 1 to 2, as said below
Outputs:
- grad_features: float32 [4096, 8, 128], P('firm', 'tm')
- grad_prev: float32 [2, 128, 256], replicated
- grad_cur: float32 [2, 128, 256], replicated
- grad_self: float32 [2, 128, 128], replicated
- grad_nbr: float32 [2, 128, 128], replicated
Inputs may be any that keep to these rules, and one draw needn't show every extreme that they name: `dilations`: each layer's dilation lies between 1 and 2; some layer has dilation 1 and some layer has dilation 2.
All inputs are finite; a program needn't handle non-finite values. No bound on the sum of `mask` on one device may be relied on, other than what follows from the above.
Results may differ from a plain program's by a relative error of at most 0.007.
Values may be sent and summed in bfloat16 or wider, within the bound.
A program may use at most 128 MiB of HBM per device.

v0:
```python
import jax
import jax.numpy as jnp
from jax import lax
from jax.sharding import PartitionSpec as P

L = 2


def shifted(array, axis, by):
    peers = lax.axis_size(axis)
    pairs = [(i, i + by) for i in range(peers) if 0 <= i + by < peers]
    return lax.ppermute(array, axis, pairs)


def earlier_time_days(hidden_state, dilation_factor):
    time_days = hidden_state.shape[1]
    prior = shifted(hidden_state, "tm", 1)
    paired_terms = jnp.concatenate([prior, hidden_state], axis=1)
    return lax.dynamic_slice_in_dim(paired_terms, time_days - dilation_factor, time_days, 1)


def later_time_days(reverse_flow, dilation_factor):
    time_days = reverse_flow.shape[1]
    following = shifted(reverse_flow, "tm", -1)
    paired_terms = jnp.concatenate([reverse_flow, following], axis=1)
    return lax.dynamic_slice_in_dim(paired_terms, dilation_factor, time_days, 1)


def folder(matrix, piece):
    return jnp.dot(matrix, piece, preferred_element_type=jnp.float32)


def per_device(features, cotangent, tiles, mask, w_prev, w_cur, w_self, w_nbr, dilations):
    rows, time_days, width = features.shape
    blocks_local, blocks_all, block_size, _ = tiles.shape
    all_firms = blocks_all * block_size
    masked = tiles * mask.astype(tiles.dtype)[:, :, None, None]
    row_matrix = masked.transpose(0, 2, 1, 3).reshape(rows, all_firms)
    saved = []
    hidden_state = features
    for layer_index in range(L):
        dilation_factor = dilations[layer_index]
        previous_state = earlier_time_days(hidden_state, dilation_factor)
        pre = jnp.dot(
            previous_state.reshape(-1, width),
            w_prev[layer_index],
            preferred_element_type=jnp.float32,
        )
        pre = pre + jnp.dot(
            hidden_state.reshape(-1, width), w_cur[layer_index], preferred_element_type=jnp.float32
        )
        filt = pre[:, :width]
        gate = pre[:, width:]
        gated = (jnp.tanh(filt) * jax.nn.sigmoid(gate)).astype(jnp.bfloat16)
        diffused = folder(
            row_matrix,
            lax.all_gather(gated.reshape(rows, time_days * width), "firm", axis=0, tiled=True),
        ).astype(jnp.bfloat16)
        mixed = jnp.dot(gated, w_self[layer_index], preferred_element_type=jnp.float32)
        mixed = mixed + jnp.dot(
            diffused.reshape(-1, width), w_nbr[layer_index], preferred_element_type=jnp.float32
        )
        saved.append((hidden_state, previous_state, filt, gate, gated, diffused))
        hidden_state = (
            hidden_state.astype(jnp.float32) + mixed.reshape(rows, time_days, width)
        ).astype(jnp.bfloat16)
    gradient_value = cotangent.astype(jnp.float32)
    outs_prev, outs_cur, outs_self, outs_nbr = ([], [], [], [])
    for layer_index in reversed(range(L)):
        hidden_state, previous_state, filt, gate, gated, diffused = saved[layer_index]
        dilation_factor = dilations[layer_index]
        gzb = gradient_value.astype(jnp.bfloat16).reshape(-1, width)
        outs_self.append(jnp.dot(gated.T, gzb, preferred_element_type=jnp.float32))
        outs_nbr.append(
            jnp.dot(diffused.reshape(-1, width).T, gzb, preferred_element_type=jnp.float32)
        )
        gdiff = jnp.dot(gzb, w_nbr[layer_index].T, preferred_element_type=jnp.float32).astype(
            jnp.bfloat16
        )
        gdiff_rows = gdiff.reshape(rows, time_days * width)
        spread = lax.psum_scatter(
            lax.dot_general(
                row_matrix, gdiff_rows, (((0,), (0,)), ((), ())), preferred_element_type=jnp.float32
            ),
            "firm",
            scatter_dimension=0,
            tiled=True,
        )
        ggated = jnp.dot(
            gzb, w_self[layer_index].T, preferred_element_type=jnp.float32
        ) + spread.reshape(-1, width)
        tanh_filt = jnp.tanh(filt)
        sig_gate = jax.nn.sigmoid(gate)
        gpre = jnp.concatenate(
            [
                ggated * sig_gate * (1.0 - tanh_filt * tanh_filt),
                ggated * tanh_filt * sig_gate * (1.0 - sig_gate),
            ],
            axis=1,
        ).astype(jnp.bfloat16)
        outs_cur.append(
            jnp.dot(hidden_state.reshape(-1, width).T, gpre, preferred_element_type=jnp.float32)
        )
        outs_prev.append(
            jnp.dot(previous_state.reshape(-1, width).T, gpre, preferred_element_type=jnp.float32)
        )
        reverse_flow = jnp.dot(
            gpre, w_prev[layer_index].T, preferred_element_type=jnp.float32
        ).reshape(rows, time_days, width)
        direct_path = jnp.dot(
            gpre, w_cur[layer_index].T, preferred_element_type=jnp.float32
        ).reshape(rows, time_days, width)
        gradient_value = (
            gradient_value + direct_path + later_time_days(reverse_flow, dilation_factor)
        )
    sums = lax.psum(
        (
            jnp.stack(outs_prev[::-1]),
            jnp.stack(outs_cur[::-1]),
            jnp.stack(outs_self[::-1]),
            jnp.stack(outs_nbr[::-1]),
        ),
        ("firm", "tm"),
    )
    factor = 1.0 / jnp.sqrt(jnp.float32(all_firms * time_days * lax.axis_size("tm")))
    return (gradient_value, sums[0] * factor, sums[1] * factor, sums[2] * factor, sums[3] * factor)


def solution(mesh):
    in_specs = (
        P("firm", "tm", None),
        P("firm", "tm", None),
        P("firm", None, None, None),
        P("firm", None),
        P(),
        P(),
        P(),
        P(),
        P(),
    )
    out_specs = (P("firm", "tm", None), P(), P(), P(), P())
    return jax.shard_map(
        per_device, mesh=mesh, in_specs=in_specs, out_specs=out_specs, check_vma=False
    )
```

profile of v0, /device:TPU:0, one launch (start us, length us, event | category | flops | bytes accessed | tf_op | source)
XLA Modules:
  0.0 454.8 jit_solution(9733607551847215862)
XLA Ops:
  7.2 2.4 collective-permute-start
  9.6 1.3 fusion.67
  12.3 1.2 fusion.39
  13.6 1.9 fusion.29
  15.5 1.2 convolution_add_fusion.1
  16.7 0.2 multiply_convert_fusion.5
  16.9 0.8 reshape.90
  17.8 2.5 multiply_bitcast_fusion
  20.4 4.7 %copy.22 = bf16[4,128,32,128]{3,2,1,0:T(8,128)(2,1)} copy(bf16[4,128,32,128]{3,1,2,0:T(8,128)(2,1)S(1)} %multiply_bitcast_fusion) | data formatting | bytes 8388608 | tf_op jit(solution)/shard_map/transpose | solution.py:38
  25.0 0.2 convolution_convert_fusion.1
  25.3 8.6 %fusion.6 = f32[4096,256]{1,0:T(8,128)} fusion(bf16[512,256]{1,0:T(8,128)(2,1)S(1)} %reshape.86, bf16[64,8,32,128]{3,2,1,0:T(8,128)(2,1)} %bitcast.128), kind=kOutput, calls=%fused_computation.6 | convolution fusion | flops 1073741824 | bytes 8650752 | tf_op jit(solution)/shard_map/dot_general | solution.py:82
  33.9 0.2 all-gather.5.cloned.1.call-start
  34.2 0.6 copy-done.13
  34.7 0.2 fusion.53
  35.0 36.5 %all-gather.3.cloned.1.call-done = bf16[4096,256]{1,0:T(8,128)(2,1)} async-done(((bf16[512,256]{1,0:T(8,128)(2,1)}), bf16[4096,256]{1,0:T(8,128)(2,1)}) %all-gather.3.cloned.1.call-update) | async-done | bytes 2097168 | tf_op jit(solution)/shard_map/all_gather | solution.py:57
  71.5 4.2 fusion.13
  75.8 0.1 reshape.91
  75.9 0.2 convolution_add_fusion.3
  76.1 0.3 add_convert_fusion
  76.4 1.3 collective-permute-start.1
  79.0 0.3 fusion.36
  79.3 1.0 fusion.28
  80.3 0.7 copy-done.5
  81.0 0.3 convolution_add_fusion
  81.2 80.5 %reduce-scatter.3.cloned.1.call-done = f32[512,256]{1,0:T(8,128)} async-done(((f32[4096,256]{1,0:T(8,128)}), f32[512,256]{1,0:T(8,128)}) %reduce-scatter.3.cloned.1.call-update) | async-done | bytes 524304 | tf_op jit(solution)/shard_map/reduce_scatter | solution.py:81
  161.7 1.9 reshape.87
  163.6 2.4 multiply_convert_fusion.3
  166.0 1.7 reshape.98
  167.8 1.0 copy_dynamic-update-slice_fusion.3
  168.8 1.0 copy_dynamic-update-slice_fusion.2
  169.8 0.3 fusion.33
  170.1 1.3 collective-permute-start.2
  173.4 0.7 collective-permute-done.2
  174.1 2.2 fusion.68
  176.3 0.3 copy.25
  176.5 1.0 convolution_convert_fusion
  177.6 8.6 %fusion.2 = f32[4096,256]{1,0:T(8,128)} fusion(bf16[512,256]{1,0:T(8,128)(2,1)S(1)} %reshape.96, bf16[64,8,32,128]{3,2,1,0:T(8,128)(2,1)} %bitcast.130), kind=kOutput, calls=%fused_computation.2 | convolution fusion | flops 1073741824 | bytes 8650752 | tf_op jit(solution)/shard_map/dot_general | solution.py:82
  186.2 0.3 all-reduce.3.cloned.1.call-start
  186.5 0.7 copy-done.7
  187.1 0.3 convolution_bitcast_fusion.6
  187.4 1.2 convolution_bitcast_fusion
  188.7 1.2 convolution_bitcast_fusion.2
  189.9 0.3 convolution_bitcast_fusion.7
  190.1 0.7 pad_maximum_fusion.8
  190.8 0.3 convolution_bitcast_fusion.5
  191.1 26.0 %all-gather.5.cloned.1.call-done = bf16[4096,256]{1,0:T(8,128)(2,1)} async-done(((bf16[512,256]{1,0:T(8,128)(2,1)}), bf16[4096,256]{1,0:T(8,128)(2,1)}) %all-gather.5.cloned.1.call-update) | async-done | bytes 2097168 | tf_op jit(solution)/shard_map/all_gather | solution.py:57
  217.1 4.2 fusion.16
  221.3 0.1 reshape.99
  221.4 0.3 convolution_bitcast_fusion.4
  221.7 0.7 pad_maximum_fusion.9
  222.4 84.9 %reduce-scatter.5.cloned.1.call-done = f32[512,256]{1,0:T(8,128)} async-done(((f32[4096,256]{1,0:T(8,128)}), f32[512,256]{1,0:T(8,128)}) %reduce-scatter.5.cloned.1.call-update) | async-done | bytes 524304 | tf_op jit(solution)/shard_map/reduce_scatter | solution.py:81
  307.3 1.1 reshape.97
  308.4 0.4 multiply_convert_fusion.1
  308.8 0.3 convolution_bitcast_fusion.1
  309.1 0.3 convolution_bitcast_fusion.3
  309.4 0.7 pad_maximum_fusion.7
  310.1 0.7 pad_maximum_fusion.6
  311.0 0.3 fusion.30
  311.3 1.3 collective-permute-start.3
  314.6 128.5 %all-reduce.3.cloned.1.call-done = (f32[2,128,256]{2,1,0:T(8,128)}, f32[2,128,256]{2,1,0:T(8,128)}, f32[2,128,128]{2,1,0:T(8,128)}, f32[2,128,128]{2,1,0:T(8,128)}) async-done(((f32[2,128,256]{2,1,0:T(8,128)}, f32[2,128,256]{2,1,0:T(8,128)}, f32[2,128,128]{2,1,0:T(8,128)}, f32[2,128,128]{2,1,0:T(8,128)}), (f32[2,128,256]{2,1,0:T(8,128)}, f32[2,128,256]{2,1,0:T(8,128)}, f32[2,128,128]{2,1,0:T(8,128)}, ...) | async-done | bytes 786448 | tf_op jit(solution)/shard_map/psum | solution.py:116
  443.1 1.7 broadcast_multiply_fusion.2
  444.8 1.9 broadcast_multiply_fusion
  446.7 0.3 fusion.12
  447.0 1.2 copy.29
  (45 shorter events, 0.6 us)
Async XLA Ops:
  7.2 10.6 %copy-start.15 = (s32[4,32]{1,0:T(4,128)S(1)}, s32[4,32]{1,0:T(4,128)}, u32[]{:S(2)}) copy-start(s32[4,32]{1,0:T(4,128)} %param.12) | copy-start | bytes 1540
  7.2 64.3 %all-gather.3.cloned.1.call-start = ((), (), s32[]{:S(2)}) async-start(), calls=%async_computation.3 | async-start | bytes 2359296 | tf_op jit(solution)/shard_map/all_gather | solution.py:57
  7.2 6.3 %collective-permute-start = (bf16[512,2,128]{2,1,0:T(2,128)(2,1)}, bf16[512,2,128]{2,1,0:T(2,128)(2,1)S(1)}, u32[]{:S(2)}, u32[]{:S(2)}) collective-permute-start(bf16[512,2,128]{2,1,0:T(2,128)(2,1)} %param.9), channel_id=1, source_target_pairs={{0,1},{1,2},{2,3},{4,5},{5,6},{6,7},{8,9},{9,10},{10,11},{12,13},{... | collective-permute-start | bytes 786440 | tf_op jit(solution)/shard_map/ppermute | solution.py:12
  15.5 1.2 copy-start.3
  17.7 144.0 %reduce-scatter.3.cloned.1.call-start = ((), (), s32[]{:S(2)}) async-start(), calls=%async_computation.2 | async-start | bytes 4718592 | tf_op jit(solution)/shard_map/reduce_scatter | solution.py:81
  20.3 4.7 %copy-start = (bf16[512,2,128]{2,1,0:T(2,128)(2,1)S(1)}, bf16[512,2,128]{2,1,0:T(2,128)(2,1)}, u32[]{:S(2)}) copy-start(bf16[512,2,128]{2,1,0:T(2,128)(2,1)} %param.10) | copy-start | bytes 786436
  20.3 4.7 %copy-start.12 = (bf16[2,128,128]{2,1,0:T(8,128)(2,1)S(1)}, bf16[2,128,128]{2,1,0:T(8,128)(2,1)}, u32[]{:S(2)}) copy-start(bf16[2,128,128]{2,1,0:T(8,128)(2,1)} %param.16) | copy-start | bytes 196612
  33.9 0.8 copy-start.13
  33.9 183.1 %all-gather.5.cloned.1.call-start = ((), (), s32[]{:S(2)}) async-start(), calls=%async_computation.5 | async-start | bytes 2359296 | tf_op jit(solution)/shard_map/all_gather | solution.py:57
  35.0 41.1 %copy-start.1 = (bf16[512,2,128]{2,1,0:T(2,128)(2,1)S(1)}, bf16[512,2,128]{2,1,0:T(2,128)(2,1)}, u32[]{:S(2)}) copy-start(bf16[512,2,128]{2,1,0:T(2,128)(2,1)} %param.9) | copy-start | bytes 786436
  35.0 44.0 %copy-start.9 = (bf16[2,128,256]{2,1,0:T(8,128)(2,1)S(1)}, bf16[2,128,256]{2,1,0:T(8,128)(2,1)}, u32[]{:S(2)}) copy-start(bf16[2,128,256]{2,1,0:T(8,128)(2,1)} %param.14) | copy-start | bytes 393220
  75.8 5.2 %copy-start.8 = (bf16[2,128,256]{2,1,0:T(8,128)(2,1)S(1)}, bf16[2,128,256]{2,1,0:T(8,128)(2,1)}, u32[]{:S(2)}) copy-start(bf16[2,128,256]{2,1,0:T(8,128)(2,1)} %param.13) | copy-start | bytes 393220
  76.4 2.9 collective-permute-start.1
  80.3 0.7 copy-start.5
  167.8 139.5 %reduce-scatter.5.cloned.1.call-start = ((), (), s32[]{:S(2)}) async-start(), calls=%async_computation.4 | async-start | bytes 4718592 | tf_op jit(solution)/shard_map/reduce_scatter | solution.py:81
  170.1 3.9 collective-permute-start.2
  186.2 1.0 copy-start.7
  186.2 1.2 copy-start.11
  186.2 2.5 copy-start.6
  186.2 256.9 %all-reduce.3.cloned.1.call-start = ((), (), s32[]{:S(2)}) async-start(), calls=%async_computation.6 | async-start | bytes 1572864 | tf_op jit(solution)/shard_map/psum | solution.py:116
  191.1 117.3 %copy-start.14 = (bf16[2,128,128]{2,1,0:T(8,128)(2,1)S(1)}, bf16[2,128,128]{2,1,0:T(8,128)(2,1)}, u32[]{:S(2)}) copy-start(bf16[2,128,128]{2,1,0:T(8,128)(2,1)} %param.15) | copy-start | bytes 196612
  221.3 87.8 %copy-start.4 = (bf16[512,2,128]{2,1,0:T(2,128)(2,1)S(1)}, bf16[512,2,128]{2,1,0:T(2,128)(2,1)}, u32[]{:S(2)}) copy-start(bf16[512,2,128]{2,1,0:T(2,128)(2,1)} %copy-done.3) | copy-start | bytes 786436
  308.8 137.9 %copy-start.2 = (f32[512,2,128]{2,0,1:T(8,128)S(1)}, f32[512,2,128]{2,0,1:T(8,128)}, u32[]{:S(2)}) copy-start(f32[512,2,128]{2,0,1:T(8,128)} %get-tuple-element.27) | copy-start | bytes 1572868
  308.8 137.9 %copy-start.10 = (bf16[2,128,256]{2,1,0:T(8,128)(2,1)S(1)}, bf16[2,128,256]{2,1,0:T(8,128)(2,1)}, u32[]{:S(2)}) copy-start(bf16[2,128,256]{2,1,0:T(8,128)(2,1)} %param.14) | copy-start | bytes 393220
  311.3 135.5 %collective-permute-start.3 = (f32[512,2,128]{2,0,1:T(8,128)S(1)}, f32[512,2,128]{2,0,1:T(8,128)S(1)}, u32[]{:S(2)}, u32[]{:S(2)}) collective-permute-start(f32[512,2,128]{2,0,1:T(8,128)S(1)} %fusion.30), channel_id=1, source_target_pairs={{1,0},{2,1},{3,2},{5,4},{6,5},{7,6},{9,8},{10,9},{11,10},{13,12},{... | collective-permute-start | bytes 1572872 | tf_op jit(solution)/shard_map/ppermute | solution.py:12
Sparse Core Ops, SparseCore 0:
  17.8 53.6 all-gather.2
  75.1 86.5 reduce-scatter.2
  167.9 49.1 all-gather.4
  221.0 86.2 reduce-scatter.4
  313.3 129.7 all-reduce.2
where the time goes:
time: 456 us; the launch traced here: 455 us
  waiting for transfers between devices  357 us (78%)
  matrix products  40.1 us (9%)
  between operations  20.9 us (5%)
  local copies, waits for them, and re-layouts  17.4 us (4%)
  other arithmetic  12.2 us (3%)
  starting transfers between devices  6.87 us (2%)
    reduce_scatter x2, waiting for transfers between devices, per_device(): lax.psum_scatter(lax.dot_general(row_matrix, gdiff_rows, (((0,), (0,)), (...  165 us
    psum x1, waiting for transfers between devices, per_device(): lax.psum((jnp.stack(outs_prev[::-1]), jnp.stack(outs_cur[::-1]), jnp.stac...  129 us
    all_gather x2, waiting for transfers between devices, per_device(): lax.all_gather(gated.reshape(rows, time_days * width), 'firm', axis=0, ti...  62.5 us
    dot_general x2, matrix products, per_device(): lax.dot_general(row_matrix, gdiff_rows, (((0,), (0,)), ((), ())), preferr...  17.1 us
  transfers between devices with their start and end apart: 9, of which 6 were waited for; matrix products, arithmetic and copies ran while one was open for 12% of the time, Pallas kernels for 0%

commit v1 on v0

v1 whole, which is shorter than its diff:
```python
import functools

import jax
import jax.numpy as jnp
from jax import lax
from jax.experimental import pallas as pl
from jax.experimental.pallas import tpu as pltpu
from jax.sharding import PartitionSpec as P

L = 2
BF = jnp.bfloat16
F32 = jnp.float32


def dot(a, b, ca=1, cb=0):
    return lax.dot_general(a, b, (((ca,), (cb,)), ((), ())), preferred_element_type=F32)


def body(n, m, short_fast, factor, x_ref, cot_ref, tiles_ref, mask_ref, wp_ref, wc_ref, ws_ref,
         wn_ref, dil_ref, gx_ref, op_ref, oc_ref, os_ref, on_ref, adj, x1, gat, th, sg, zt, acc, gx,
         prv, gpre, halo, back, nxt, ag_r, ag_l, rs_out, rs_in, gp, r1, s2, fin, send, recv):
    rows, wide = x_ref.shape
    c = wide // 2
    half = n // 2
    f = lax.axis_index("firm")
    t = lax.axis_index("tm")
    if short_fast:
        fy, fz = f % 2, f // 2
    else:
        fy, fz = f // half, f % half
    pos = fz + fy * (n - 1 - 2 * fz)

    def firm_at(p):
        p = (p + 2 * n) % n
        y = p // half
        z = p + y * (n - 1 - 2 * p)
        return 2 * z + y if short_fast else y * half + z

    right = firm_at(pos + 1)
    left = firm_at(pos - 1)
    later = (t + 1) % m
    sooner = (t + m - 1) % m
    started = []

    def copy(src, dst, firm=None, tm=None):
        i = len(started)
        cp = pltpu.make_async_remote_copy(
            src_ref=src, dst_ref=dst, send_sem=send.at[i], recv_sem=recv.at[i],
            device_id=(f if firm is None else firm, t if tm is None else tm),
            device_id_type=pl.DeviceIdType.MESH)
        cp.start()
        started.append(cp)
        return cp

    barrier = pltpu.get_barrier_semaphore()
    for o in range(1, n):
        pl.semaphore_signal(barrier, inc=1, device_id=((f + o) % n, t),
                            device_id_type=pl.DeviceIdType.MESH)
    for o in range(1, m):
        pl.semaphore_signal(barrier, inc=1, device_id=(f, (t + o) % m),
                            device_id_type=pl.DeviceIdType.MESH)
    pl.semaphore_wait(barrier, n + m - 2)

    def day(k):
        return slice(k * c, (k + 1) * c)

    def block(q):
        return pl.ds(pl.multiple_of(firm_at(q) * rows, rows), rows)

    halo_cp = copy(x_ref, halo.at[0], tm=later)

    def build(j, _):
        cols = pl.ds(pl.multiple_of(j * c, c), c)
        for i in range(tiles_ref.shape[0]):
            keep = mask_ref[i, j].astype(F32)
            adj[i * c:(i + 1) * c, cols] = (tiles_ref[i, j].astype(F32) * keep).astype(BF)
        return 0

    lax.fori_loop(0, tiles_ref.shape[1], build, 0)

    class Scatter:
        def __init__(self, w):
            self.w, self.cps = w, []

        def part(self, q):
            return dot(zt[self.w], adj[:, block(q)])

        def begin(self):
            p = self.part(pos + half).astype(BF)
            out = rs_out.at[self.w, 0, 0]
            out[...] = p
            top, low = pl.ds(0, c), pl.ds(c, c)
            self.cps.append((
                copy(out.at[top], rs_in.at[self.w, 0, 0, top], firm=right),
                copy(out.at[low], rs_in.at[self.w, 1, 0, low], firm=left)))

        def step(self, k):
            new = []
            for dr in range(2):
                p = self.part(pos + (half - k) * (1 - 2 * dr))
                self.cps[k - 1][dr].wait_recv()
                out = rs_out.at[self.w, dr, k]
                if k == 1:
                    got = slice(dr * c, (dr + 1) * c)
                    own = slice((1 - dr) * c, (2 - dr) * c)
                    out[got, :] = (p[got] + rs_in[self.w, dr, 0, got].astype(F32)).astype(BF)
                    out[own, :] = p[own].astype(BF)
                else:
                    out[...] = (p + rs_in[self.w, dr, k - 1].astype(F32)).astype(BF)
                new.append(copy(out, rs_in.at[self.w, dr, k], firm=(right, left)[dr]))
            self.cps.append(new)

        def end(self):
            p = self.part(pos)
            for dr in range(2):
                self.cps[half - 1][dr].wait_recv()
                p = p + rs_in[self.w, dr, half - 1].astype(F32)
            return p.T.astype(BF)

    def forward(l, x):
        d1 = dil_ref[l] == 1
        h = halo[l].astype(F32)
        h = h * jnp.where(t > 0, 1.0, 0.0)
        one = jnp.where(d1, 1.0, 0.0)
        h0, h1 = h[:, day(0)], h[:, day(1)]
        prv[l, :, day(0)] = (h1 * one + h0 * (1.0 - one)).astype(BF)
        prv[l, :, day(1)] = (x[:, day(0)].astype(F32) * one + h1 * (1.0 - one)).astype(BF)
        for k in range(2):
            pre = dot(prv[l, :, day(k)], wp_ref[l]) + dot(x[:, day(k)], wc_ref[l])
            a = jnp.tanh(pre[:, :c])
            b = 0.5 * jnp.tanh(0.5 * pre[:, c:]) + 0.5
            th[l, :, day(k)] = a
            sg[l, :, day(k)] = b
            gat[l, :, day(k)] = (a * b).astype(BF)

    def pre_grad(l, zb, u):
        for k in range(2):
            gg = dot(zb[:, day(k)], ws_ref[l], 1, 1) + dot(u[:, day(k)], wn_ref[l], 1, 1)
            a, b = th[l, :, day(k)], sg[l, :, day(k)]
            gpre[k, :, :c] = (gg * b * (1.0 - a * a)).astype(BF)
            gpre[k, :, c:] = (gg * a * b * (1.0 - b)).astype(BF)
            back[l, :, day(k)] = dot(gpre[k], wp_ref[l], 1, 1).astype(BF)

    def direct(l, k):
        return dot(gpre[k], wc_ref[l], 1, 1)

    def shifted(l):
        one = jnp.where(dil_ref[l] == 1, 1.0, 0.0)
        nb = nxt[l].astype(F32) * jnp.where(t < m - 1, 1.0, 0.0)
        n0, n1 = nb[:, day(0)], nb[:, day(1)]
        b1 = back[l, :, day(1)].astype(F32)
        return (b1 * one + n0 * (1.0 - one), n0 * one + n1 * (1.0 - one))

    def weight_grads(l, x, zb, u):
        def total(a, b):
            return dot(a[:, day(0)], b[0], 0, 0) + dot(a[:, day(1)], b[1], 0, 0)

        pieces = []
        g2 = (gpre[0], gpre[1])
        for w in (total(prv[l], g2), total(x, g2)):
            pieces += [w[:, :c], w[:, c:]]
        z2 = (zb[:, day(0)], zb[:, day(1)])
        u2 = (u[:, day(0)], u[:, day(1)])
        pieces += [total(gat[l], z2), total(gat[l], u2)]
        gp[l] = jnp.concatenate(pieces, axis=0).astype(BF).reshape(gp.shape[1:])

    class Total:
        def __init__(self, l):
            self.l = l

        def first(self):
            self.a = [copy(gp.at[self.l, (f + o) % n], r1.at[self.l, o - 1], firm=(f + o) % n)
                      for o in range(1, n)]

        def second(self):
            l = self.l
            s = gp[l, f].astype(F32)
            for o in range(1, n):
                self.a[o - 1].wait_recv()
                s = s + r1[l, o - 1].astype(F32)
            s2[l, t] = s.astype(BF)
            self.b = [copy(s2.at[l, t], s2.at[l, t], tm=(t + o) % m) for o in range(1, m)]

        def third(self):
            l = self.l
            for cp in self.b:
                cp.wait_recv()
            s = s2[l, 0].astype(F32)
            for j in range(1, m):
                s = s + s2[l, j].astype(F32)
            fin[l, f] = s.astype(BF)
            self.d = [copy(fin.at[l, f], fin.at[l, f], firm=(f + o) % n) for o in range(1, n)]

        def last(self):
            l = self.l
            for cp in self.d:
                cp.wait_recv()
            g = fin[l].reshape(6 * c, c).astype(F32) * factor
            op_ref[l, :, :c] = g[:c]
            op_ref[l, :, c:] = g[c:2 * c]
            oc_ref[l, :, :c] = g[2 * c:3 * c]
            oc_ref[l, :, c:] = g[3 * c:4 * c]
            os_ref[l] = g[4 * c:5 * c]
            on_ref[l] = g[5 * c:]

    zt[1] = cot_ref[...].astype(F32).T.astype(BF)
    rs1 = Scatter(1)
    rs1.begin()
    halo_cp.wait_recv()
    x0 = x_ref[...]
    forward(0, x0)

    cps = [(copy(gat.at[0], ag_r.at[0], firm=right), copy(gat.at[0], ag_l.at[0], firm=left))]
    acc[...] = dot(adj[:, block(pos)], gat[0])
    for s in range(1, half + 1):
        new = []
        for dr, (buf, to) in enumerate(((ag_r, right), (ag_l, left))):
            cps[s - 1][dr].wait_recv()
            if s < half - 1:
                new.append(copy(buf.at[s - 1], buf.at[s], firm=to))
            elif s == half - 1:
                part = pl.ds(dr * (rows // 2), rows // 2)
                new.append(copy(buf.at[s - 1, part], buf.at[s, part], firm=to))
        cps.append(new)
        if s < half:
            acc[...] += (dot(adj[:, block(pos - s)], ag_r[s - 1])
                         + dot(adj[:, block(pos + s)], ag_l[s - 1]))
            if s < half - 1:
                rs1.step(s)
        else:
            h = rows // 2
            far = firm_at(pos + half) * rows
            acc[...] += (dot(adj[:, pl.ds(pl.multiple_of(far, h), h)], ag_r[s - 1, :h])
                         + dot(adj[:, pl.ds(pl.multiple_of(far + h, h), h)], ag_l[s - 1, h:]))
    for k in range(2):
        mixed = (dot(gat[0, :, day(k)], ws_ref[0])
                 + dot(acc[:, day(k)].astype(BF), wn_ref[0]))
        x1[:, day(k)] = (x_ref[:, day(k)].astype(F32) + mixed).astype(BF)
    halo_cp = copy(x1, halo.at[1], tm=later)
    rs1.step(half - 1)
    halo_cp.wait_recv()
    forward(1, x1[...])

    cot = cot_ref[...]
    u = rs1.end()
    pre_grad(1, cot, u)
    back_cp = copy(back.at[1], nxt.at[1], tm=sooner)
    weight_grads(1, x1[...], cot, u)
    for k in range(2):
        gx[:, day(k)] = cot[:, day(k)].astype(F32) + direct(1, k)
    back_cp.wait_recv()
    sh = shifted(1)
    for k in range(2):
        gx[:, day(k)] = gx[:, day(k)] + sh[k]
    zb = gx[...].astype(BF)
    zt[0] = gx[...].T.astype(BF)
    rs0 = Scatter(0)
    rs0.begin()
    sum1 = Total(1)
    sum1.first()
    for k in range(1, half):
        rs0.step(k)
        if k == 1:
            sum1.second()
        if k == 2:
            sum1.third()
    u = rs0.end()
    pre_grad(0, zb, u)
    back_cp = copy(back.at[0], nxt.at[0], tm=sooner)
    weight_grads(0, x0, zb, u)
    sum0 = Total(0)
    sum0.first()
    for k in range(2):
        gx[:, day(k)] = gx[:, day(k)] + direct(0, k)
    sum0.second()
    back_cp.wait_recv()
    sh = shifted(0)
    for k in range(2):
        gx_ref[:, day(k)] = gx[:, day(k)] + sh[k]
    sum0.third()
    sum1.last()
    sum0.last()
    for cp in started:
        cp.wait_send()


def per_device(n, m, features, cotangent, tiles, mask, w_prev, w_cur, w_self, w_nbr, dilations):
    rows, days, c = features.shape
    wide = days * c
    half = n // 2
    share = 6 * c // n
    factor = 1.0 / float(rows * n * days * m) ** 0.5
    copies = 4 + 6 * half + 2 * (2 * (n - 1) + m - 1)
    vm = pl.BlockSpec(memory_space=pltpu.VMEM)
    sm = pl.BlockSpec(memory_space=pltpu.SMEM)
    outs = pl.pallas_call(
        functools.partial(body, n, m, n == 8, factor),
        out_shape=[
            jax.ShapeDtypeStruct((rows, wide), F32),
            jax.ShapeDtypeStruct(w_prev.shape, F32),
            jax.ShapeDtypeStruct(w_cur.shape, F32),
            jax.ShapeDtypeStruct(w_self.shape, F32),
            jax.ShapeDtypeStruct(w_nbr.shape, F32),
        ],
        in_specs=[vm, vm, vm, sm, vm, vm, vm, vm, sm],
        out_specs=[vm] * 5,
        scratch_shapes=[
            pltpu.VMEM((rows, rows * n), BF),
            pltpu.VMEM((rows, wide), BF),
            pltpu.VMEM((L, rows, wide), BF),
            pltpu.VMEM((L, rows, wide), F32),
            pltpu.VMEM((L, rows, wide), F32),
            pltpu.VMEM((L, wide, rows), BF),
            pltpu.VMEM((rows, wide), F32),
            pltpu.VMEM((rows, wide), F32),
            pltpu.VMEM((L, rows, wide), BF),
            pltpu.VMEM((2, rows, 2 * c), BF),
            pltpu.VMEM((L, rows, wide), BF),
            pltpu.VMEM((L, rows, wide), BF),
            pltpu.VMEM((L, rows, wide), BF),
            pltpu.VMEM((half, rows, wide), BF),
            pltpu.VMEM((half, rows, wide), BF),
            pltpu.VMEM((L, 2, half, wide, rows), BF),
            pltpu.VMEM((L, 2, half, wide, rows), BF),
            pltpu.VMEM((L, n, share, c), BF),
            pltpu.VMEM((L, n - 1, share, c), BF),
            pltpu.VMEM((L, m, share, c), BF),
            pltpu.VMEM((L, n, share, c), BF),
            pltpu.SemaphoreType.DMA((copies,)),
            pltpu.SemaphoreType.DMA((copies,)),
        ],
        compiler_params=pltpu.CompilerParams(
            collective_id=0, has_side_effects=True, vmem_limit_bytes=60 * 1024 * 1024),
        name="wavenet_backward",
    )(features.reshape(rows, wide), cotangent.reshape(rows, wide), tiles, mask, w_prev, w_cur,
      w_self, w_nbr, dilations)
    return (outs[0].reshape(rows, days, c), *outs[1:])


def solution(mesh):
    in_specs = (
        P("firm", "tm", None),
        P("firm", "tm", None),
        P("firm", None, None, None),
        P("firm", None),
        P(),
        P(),
        P(),
        P(),
        P(),
    )
    out_specs = (P("firm", "tm", None), P(), P(), P(), P())
    return jax.shard_map(
        functools.partial(per_device, mesh.shape["firm"], mesh.shape["tm"]),
        mesh=mesh, in_specs=in_specs, out_specs=out_specs, check_vma=False
    )
```

time: 456 us -> 114 us (0.25)
  waiting for transfers between devices: 357 us -> 0 us
  Pallas kernels: 0 us -> 103 us
  matrix products: 40.1 us -> 0 us
  between operations: 20.9 us -> 0.64 us
  other arithmetic: 12.2 us -> 0 us
  local copies, waits for them, and re-layouts: 17.4 us -> 10.5 us
  starting transfers between devices: 6.87 us -> 0 us
    reduce_scatter x2 -> x0, waiting for transfers between devices: 165 us -> none  [per_device(): lax.psum_scatter(lax.dot_general(row_matrix, gdiff_rows, (((0,), (0,)), (...]
    psum x1 -> x0, waiting for transfers between devices: 129 us -> none  [per_device(): lax.psum((jnp.stack(outs_prev[::-1]), jnp.stack(outs_cur[::-1]), jnp.stac...]
    pallas_call x0 -> x1, Pallas kernels: none -> 103 us  [per_device(): pl.pallas_call(functools.partial(body, n, m, n == 8, factor), out_shape=[...]
    all_gather x2 -> x0, waiting for transfers between devices: 62.5 us -> none  [per_device(): lax.all_gather(gated.reshape(rows, time_days * width), 'firm', axis=0, ti...]
    dot_general x26 -> x0, matrix products: 40.1 us -> none  [the longest x2 17.1 us: per_device(): lax.dot_general(row_matrix, gdiff_rows, (((0,), (0,)), ((), ())), preferr...]
    ppermute x4 -> x0, starting transfers between devices: 6.26 us -> none  [shifted(): return lax.ppermute(array, axis, pairs)]
    transpose x1 -> x0, local copies, waits for them, and re-layouts: 4.66 us -> none  [per_device(): row_matrix = masked.transpose(0, 2, 1, 3).reshape(rows, all_firms)]
  transfers between devices with their start and end apart: 9 -> 0, of which waited for: 6 -> 0; matrix products, arithmetic and copies ran while one was open for 12% -> 0% of each run, Pallas kernels for 0% -> 0%
where the time goes in v1:
time: 114 us
  Pallas kernels  103 us (90%)
  local copies, waits for them, and re-layouts  10.5 us (9%)
    pallas_call x1, Pallas kernels, per_device(): pl.pallas_call(functools.partial(body, n, m, n == 8, factor), out_shape=[...  103 us
    unnamed x4, local copies, waits for them, and re-layouts  6.47 us

profile of v1, /device:TPU:0, one launch (start us, length us, event | category | flops | bytes accessed | tf_op | source)
XLA Modules:
  0.0 114.0 jit_solution(1723969543768866657)
XLA Ops:
  0.6 1.9 %copy_bitcast_fusion = (bf16[512,256]{1,0:T(8,128)(2,1)}, bf16[512,256]{1,0:T(8,128)(2,1)}) fusion(bf16[64,8,2,128]{3,2,1,0:T(2,128)(2,1)} %bitcast.6, bf16[64,8,2,128]{3,2,1,0:T(2,128)(2,1)} %bitcast.7), kind=kLoop, calls=%fused_computation | loop fusion | bytes 1048576 | tf_op jit(solution)/shard_map/reshape | solution.py:335
  2.5 102.9 %wavenet_backward.1 = (f32[512,256]{1,0:T(8,128)}, f32[2,128,256]{2,1,0:T(8,128)}, f32[2,128,256]{2,1,0:T(8,128)}, f32[2,128,128]{2,1,0:T(8,128)}, f32[2,128,128]{2,1,0:T(8,128)}) custom-call(bf16[512,256]{1,0:T(8,128)(2,1)} %get-tuple-element.16.x_ref, bf16[512,256]{1,0:T(8,128)(2,1)} %get-tuple-element.15.cot_ref, bf16[4,32,128,128]{3,2,1,0:T(8,128)(2,1)} %tiles_ref.1, ...), custom_call_target="tpu_custom_call" | custom-call | tf_op jit(solution)/shard_map/wavenet_backward/pallas_call | solution.py:296
  105.4 2.1 %reshape.21 = f32[512,2,128]{2,1,0:T(2,128)} reshape(f32[512,256]{1,0:T(8,128)} %get-tuple-element.10) | data formatting | bytes 1048576 | tf_op jit(solution)/shard_map/reshape | solution.py:337
  107.5 1.7 %copy.22 = f32[2,128,256]{2,1,0:T(8,128)} copy(f32[2,128,256]{2,1,0:T(8,128)} %get-tuple-element.23) | data formatting | bytes 524288
  109.2 1.7 %copy.23 = f32[2,128,256]{2,1,0:T(8,128)} copy(f32[2,128,256]{2,1,0:T(8,128)} %get-tuple-element.24) | data formatting | bytes 524288
  110.8 1.6 %copy.24 = f32[2,128,128]{2,1,0:T(8,128)} copy(f32[2,128,128]{2,1,0:T(8,128)} %get-tuple-element.25) | data formatting | bytes 262144
  112.4 1.6 %copy.25 = f32[2,128,128]{2,1,0:T(8,128)} copy(f32[2,128,128]{2,1,0:T(8,128)} %get-tuple-element.26) | data formatting | bytes 262144

commit v2 on v1

--- a/solution.py
+++ b/solution.py
@@ -16,8 +16,8 @@
     return lax.dot_general(a, b, (((ca,), (cb,)), ((), ())), preferred_element_type=F32)
 
 
-def body(n, m, short_fast, factor, x_ref, cot_ref, tiles_ref, mask_ref, wp_ref, wc_ref, ws_ref,
-         wn_ref, dil_ref, gx_ref, op_ref, oc_ref, os_ref, on_ref, adj, x1, gat, th, sg, zt, acc, gx,
+def body(n, m, short_fast, x_ref, cot_ref, tiles_ref, mask_ref, wp_ref, wc_ref, ws_ref,
+         wn_ref, dil_ref, gx_ref, sum_ref, adj, x1, gat, th, sg, zt, acc, acc_t, uu, gx, cur,
          prv, gpre, halo, back, nxt, ag_r, ag_l, rs_out, rs_in, gp, r1, s2, fin, send, recv):
     rows, wide = x_ref.shape
     c = wide // 2
@@ -59,7 +59,6 @@
     for o in range(1, m):
         pl.semaphore_signal(barrier, inc=1, device_id=(f, (t + o) % m),
                             device_id_type=pl.DeviceIdType.MESH)
-    pl.semaphore_wait(barrier, n + m - 2)
 
     def day(k):
         return slice(k * c, (k + 1) * c)
@@ -67,55 +66,54 @@
     def block(q):
         return pl.ds(pl.multiple_of(firm_at(q) * rows, rows), rows)
 
-    halo_cp = copy(x_ref, halo.at[0], tm=later)
-
-    def build(j, _):
-        cols = pl.ds(pl.multiple_of(j * c, c), c)
-        for i in range(tiles_ref.shape[0]):
-            keep = mask_ref[i, j].astype(F32)
-            adj[i * c:(i + 1) * c, cols] = (tiles_ref[i, j].astype(F32) * keep).astype(BF)
-        return 0
-
-    lax.fori_loop(0, tiles_ref.shape[1], build, 0)
+    def build(q):
+        first = firm_at(q) * (rows // c)
+
+        def one(j, _):
+            cols = pl.ds(pl.multiple_of((first + j) * c, c), c)
+            for i in range(rows // c):
+                keep = mask_ref[i, first + j].astype(F32).astype(BF)
+                adj[i * c:(i + 1) * c, cols] = tiles_ref[i, first + j] * keep
+            return 0
+
+        lax.fori_loop(0, rows // c, one, 0)
 
     class Scatter:
         def __init__(self, w):
-            self.w, self.cps = w, []
-
-        def part(self, q):
-            return dot(zt[self.w], adj[:, block(q)])
-
-        def begin(self):
-            p = self.part(pos + half).astype(BF)
-            out = rs_out.at[self.w, 0, 0]
-            out[...] = p
-            top, low = pl.ds(0, c), pl.ds(c, c)
-            self.cps.append((
-                copy(out.at[top], rs_in.at[self.w, 0, 0, top], firm=right),
-                copy(out.at[low], rs_in.at[self.w, 1, 0, low], firm=left)))
-
-        def step(self, k):
-            new = []
+            self.w, self.cps = w, {}
+
+        def send(self, dr, k, which):
+            sign = 1 - 2 * dr
+            p = dot(zt[self.w, day(which)], adj[:, block(pos + (half - k) * sign)])
+            if (dr, k - 1, which) in self.cps:
+                self.cps[dr, k - 1, which].wait_recv()
+                p = p + rs_in[self.w, dr, k - 1, day(which)].astype(F32)
+            rs_out[self.w, dr, k, day(which)] = p.astype(BF)
+            part = pl.ds(which * c, c)
+            self.cps[dr, k, which] = copy(
+                rs_out.at[self.w, dr, k, part], rs_in.at[self.w, dr, k, part],
+                firm=(right, left)[dr])
+
+        def round(self, r):
             for dr in range(2):
-                p = self.part(pos + (half - k) * (1 - 2 * dr))
-                self.cps[k - 1][dr].wait_recv()
-                out = rs_out.at[self.w, dr, k]
-                if k == 1:
-                    got = slice(dr * c, (dr + 1) * c)
-                    own = slice((1 - dr) * c, (2 - dr) * c)
-                    out[got, :] = (p[got] + rs_in[self.w, dr, 0, got].astype(F32)).astype(BF)
-                    out[own, :] = p[own].astype(BF)
-                else:
-                    out[...] = (p + rs_in[self.w, dr, k - 1].astype(F32)).astype(BF)
-                new.append(copy(out, rs_in.at[self.w, dr, k], firm=(right, left)[dr]))
-            self.cps.append(new)
-
-        def end(self):
-            p = self.part(pos)
+                self.send(dr, r, dr)
+            if r + 1 < half:
+                for dr in range(2):
+                    self.send(dr, r + 1, 1 - dr)
+
+        def own(self):
+            acc_t[...] = dot(zt[self.w], adj[:, block(pos)])
+
+        def end(self, k):
+            p = acc_t[day(k)]
             for dr in range(2):
-                self.cps[half - 1][dr].wait_recv()
-                p = p + rs_in[self.w, dr, half - 1].astype(F32)
-            return p.T.astype(BF)
+                self.cps[dr, half - 1, k].wait_recv()
+                p = p + rs_in[self.w, dr, half - 1, day(k)].astype(F32)
+            uu[:, day(k)] = p.T.astype(BF)
+
+    def current(l, x):
+        for k in range(2):
+            cur[k] = dot(x[:, day(k)], wc_ref[l])
 
     def forward(l, x):
         d1 = dil_ref[l] == 1
@@ -126,16 +124,18 @@
         prv[l, :, day(0)] = (h1 * one + h0 * (1.0 - one)).astype(BF)
         prv[l, :, day(1)] = (x[:, day(0)].astype(F32) * one + h1 * (1.0 - one)).astype(BF)
         for k in range(2):
-            pre = dot(prv[l, :, day(k)], wp_ref[l]) + dot(x[:, day(k)], wc_ref[l])
+            pre = dot(prv[l, :, day(k)], wp_ref[l]) + cur[k]
             a = jnp.tanh(pre[:, :c])
             b = 0.5 * jnp.tanh(0.5 * pre[:, c:]) + 0.5
             th[l, :, day(k)] = a
             sg[l, :, day(k)] = b
             gat[l, :, day(k)] = (a * b).astype(BF)
 
-    def pre_grad(l, zb, u):
+    def pre_grad(l, zb, scatter):
         for k in range(2):
-            gg = dot(zb[:, day(k)], ws_ref[l], 1, 1) + dot(u[:, day(k)], wn_ref[l], 1, 1)
+            gg = dot(zb[:, day(k)], ws_ref[l], 1, 1)
+            scatter.end(k)
+            gg = gg + dot(uu[:, day(k)], wn_ref[l], 1, 1)
             a, b = th[l, :, day(k)], sg[l, :, day(k)]
             gpre[k, :, :c] = (gg * b * (1.0 - a * a)).astype(BF)
             gpre[k, :, c:] = (gg * a * b * (1.0 - b)).astype(BF)
@@ -195,23 +195,25 @@
             l = self.l
             for cp in self.d:
                 cp.wait_recv()
-            g = fin[l].reshape(6 * c, c).astype(F32) * factor
-            op_ref[l, :, :c] = g[:c]
-            op_ref[l, :, c:] = g[c:2 * c]
-            oc_ref[l, :, :c] = g[2 * c:3 * c]
-            oc_ref[l, :, c:] = g[3 * c:4 * c]
-            os_ref[l] = g[4 * c:5 * c]
-            on_ref[l] = g[5 * c:]
+            sum_ref[l] = fin[l].reshape(6 * c, c)
 
     zt[1] = cot_ref[...].astype(F32).T.astype(BF)
+    for q in (half, half - 1, 1 - half):
+        build(pos + q)
+    pl.semaphore_wait(barrier, n + m - 2)
+    halo_cp = copy(x_ref, halo.at[0], tm=later)
     rs1 = Scatter(1)
-    rs1.begin()
+    rs1.round(0)
+    x0 = x_ref[...]
+    current(0, x0)
+    for q in range(2 - half, half - 1):
+        build(pos + q)
     halo_cp.wait_recv()
-    x0 = x_ref[...]
     forward(0, x0)
 
     cps = [(copy(gat.at[0], ag_r.at[0], firm=right), copy(gat.at[0], ag_l.at[0], firm=left))]
     acc[...] = dot(adj[:, block(pos)], gat[0])
+    rs1.round(1)
     for s in range(1, half + 1):
         new = []
         for dr, (buf, to) in enumerate(((ag_r, right), (ag_l, left))):
@@ -225,8 +227,10 @@
         if s < half:
             acc[...] += (dot(adj[:, block(pos - s)], ag_r[s - 1])
                          + dot(adj[:, block(pos + s)], ag_l[s - 1]))
-            if s < half - 1:
-                rs1.step(s)
+            if s < half - 2:
+                rs1.round(s + 1)
+            elif s == half - 1:
+                rs1.round(s)
         else:
             h = rows // 2
             far = firm_at(pos + half) * rows
@@ -237,17 +241,17 @@
                  + dot(acc[:, day(k)].astype(BF), wn_ref[0]))
         x1[:, day(k)] = (x_ref[:, day(k)].astype(F32) + mixed).astype(BF)
     halo_cp = copy(x1, halo.at[1], tm=later)
-    rs1.step(half - 1)
+    current(1, x1[...])
+    rs1.own()
     halo_cp.wait_recv()
     forward(1, x1[...])
 
     cot = cot_ref[...]
-    u = rs1.end()
-    pre_grad(1, cot, u)
+    pre_grad(1, cot, rs1)
     back_cp = copy(back.at[1], nxt.at[1], tm=sooner)
-    weight_grads(1, x1[...], cot, u)
     for k in range(2):
         gx[:, day(k)] = cot[:, day(k)].astype(F32) + direct(1, k)
+    weight_grads(1, x1[...], cot, uu[...])
     back_cp.wait_recv()
     sh = shifted(1)
     for k in range(2):
@@ -255,19 +259,19 @@
     zb = gx[...].astype(BF)
     zt[0] = gx[...].T.astype(BF)
     rs0 = Scatter(0)
-    rs0.begin()
+    rs0.round(0)
     sum1 = Total(1)
     sum1.first()
+    rs0.own()
     for k in range(1, half):
-        rs0.step(k)
+        rs0.round(k)
         if k == 1:
             sum1.second()
         if k == 2:
             sum1.third()
-    u = rs0.end()
-    pre_grad(0, zb, u)
+    pre_grad(0, zb, rs0)
     back_cp = copy(back.at[0], nxt.at[0], tm=sooner)
-    weight_grads(0, x0, zb, u)
+    weight_grads(0, x0, zb, uu[...])
     sum0 = Total(0)
     sum0.first()
     for k in range(2):
@@ -284,26 +288,37 @@
         cp.wait_send()
 
 
+def finish(factor, gx_ref, sum_ref, out_ref, op_ref, oc_ref, os_ref, on_ref):
+    c = on_ref.shape[-1]
+    for k in range(2):
+        out_ref[:, k, :] = gx_ref[:, k * c:(k + 1) * c]
+    for l in range(L):
+        g = sum_ref[l].astype(F32) * factor
+        op_ref[l, :, :c] = g[:c]
+        op_ref[l, :, c:] = g[c:2 * c]
+        oc_ref[l, :, :c] = g[2 * c:3 * c]
+        oc_ref[l, :, c:] = g[3 * c:4 * c]
+        os_ref[l] = g[4 * c:5 * c]
+        on_ref[l] = g[5 * c:]
+
+
 def per_device(n, m, features, cotangent, tiles, mask, w_prev, w_cur, w_self, w_nbr, dilations):
     rows, days, c = features.shape
     wide = days * c
     half = n // 2
     share = 6 * c // n
     factor = 1.0 / float(rows * n * days * m) ** 0.5
-    copies = 4 + 6 * half + 2 * (2 * (n - 1) + m - 1)
+    copies = 4 + 2 * half + 4 * (n - 1) + 2 * (2 * (n - 1) + m - 1)
     vm = pl.BlockSpec(memory_space=pltpu.VMEM)
     sm = pl.BlockSpec(memory_space=pltpu.SMEM)
-    outs = pl.pallas_call(
-        functools.partial(body, n, m, n == 8, factor),
+    flow, sums = pl.pallas_call(
+        functools.partial(body, n, m, n == 8),
         out_shape=[
             jax.ShapeDtypeStruct((rows, wide), F32),
-            jax.ShapeDtypeStruct(w_prev.shape, F32),
-            jax.ShapeDtypeStruct(w_cur.shape, F32),
-            jax.ShapeDtypeStruct(w_self.shape, F32),
-            jax.ShapeDtypeStruct(w_nbr.shape, F32),
+            jax.ShapeDtypeStruct((L, 6 * c, c), BF),
         ],
         in_specs=[vm, vm, vm, sm, vm, vm, vm, vm, sm],
-        out_specs=[vm] * 5,
+        out_specs=[vm] * 2,
         scratch_shapes=[
             pltpu.VMEM((rows, rows * n), BF),
             pltpu.VMEM((rows, wide), BF),
@@ -312,7 +327,10 @@
             pltpu.VMEM((L, rows, wide), F32),
             pltpu.VMEM((L, wide, rows), BF),
             pltpu.VMEM((rows, wide), F32),
+            pltpu.VMEM((wide, rows), F32),
+            pltpu.VMEM((rows, wide), BF),
             pltpu.VMEM((rows, wide), F32),
+            pltpu.VMEM((2, rows, 2 * c), F32),
             pltpu.VMEM((L, rows, wide), BF),
             pltpu.VMEM((2, rows, 2 * c), BF),
             pltpu.VMEM((L, rows, wide), BF),
@@ -334,7 +352,19 @@
         name="wavenet_backward",
     )(features.reshape(rows, wide), cotangent.reshape(rows, wide), tiles, mask, w_prev, w_cur,
       w_self, w_nbr, dilations)
-    return (outs[0].reshape(rows, days, c), *outs[1:])
+    return pl.pallas_call(
+        functools.partial(finish, factor),
+        out_shape=[
+            jax.ShapeDtypeStruct(features.shape, F32),
+            jax.ShapeDtypeStruct(w_prev.shape, F32),
+            jax.ShapeDtypeStruct(w_cur.shape, F32),
+            jax.ShapeDtypeStruct(w_self.shape, F32),
+            jax.ShapeDtypeStruct(w_nbr.shape, F32),
+        ],
+        in_specs=[vm] * 2,
+        out_specs=[vm] * 5,
+        name="finish",
+    )(flow, sums)
 
 
 def solution(mesh):

time: 114 us -> 106 us (0.930)
  local copies, waits for them, and re-layouts: 10.5 us -> 1.89 us
    unnamed x4 -> x0, local copies, waits for them, and re-layouts: 6.47 us -> none
    reshape x1 -> x0, local copies, waits for them, and re-layouts: 2.09 us -> none  [per_device(): return (outs[0].reshape(rows, days, c), *outs[1:])]
    pallas_call x1 -> x2, Pallas kernels: 103 us -> 103 us  [the longest x1 101 us: per_device(): pl.pallas_call(functools.partial(body, n, m, n == 8), out_shape=[jax.Shap...]
where the time goes in v2:
time: 106 us
  Pallas kernels  103 us (97%)
  local copies, waits for them, and re-layouts  1.89 us (2%)
    pallas_call x1, Pallas kernels, per_device(): pl.pallas_call(functools.partial(body, n, m, n == 8), out_shape=[jax.Shap...  101 us
    pallas_call x1, Pallas kernels, per_device(): pl.pallas_call(functools.partial(finish, factor), out_shape=[jax.ShapeDty...  2.39 us

profile of v2, /device:TPU:0, one launch (start us, length us, event | category | flops | bytes accessed | tf_op | source)
XLA Modules:
  0.0 106.0 jit_solution(8708761003423380702)
XLA Ops:
  0.6 1.9 %copy_bitcast_fusion = (bf16[512,256]{1,0:T(8,128)(2,1)}, bf16[512,256]{1,0:T(8,128)(2,1)}) fusion(bf16[64,8,2,128]{3,2,1,0:T(2,128)(2,1)} %bitcast.6, bf16[64,8,2,128]{3,2,1,0:T(2,128)(2,1)} %bitcast.7), kind=kLoop, calls=%fused_computation | loop fusion | bytes 1048576 | tf_op jit(solution)/shard_map/reshape | solution.py:353
  2.5 101.1 %wavenet_backward.1 = (f32[512,256]{1,0:T(8,128)}, bf16[2,768,128]{2,1,0:T(8,128)(2,1)}) custom-call(bf16[512,256]{1,0:T(8,128)(2,1)} %get-tuple-element.10.x_ref, bf16[512,256]{1,0:T(8,128)(2,1)} %get-tuple-element.9.cot_ref, bf16[4,32,128,128]{3,2,1,0:T(8,128)(2,1)} %tiles_ref.1, s32[4,32]{1,0:T(4,128)} %mask_ref.1, bf16[2,128,256]{2,1,0:T(8,128)(2,1)} %wp_ref.1, ...), custom_call_target="tpu_custom_call" | custom-call | tf_op jit(solution)/shard_map/wavenet_backward/pallas_call | solution.py:314
  103.6 2.4 %finish.1 = (f32[512,2,128]{2,1,0:T(2,128)}, f32[2,128,256]{2,1,0:T(8,128)}, f32[2,128,256]{2,1,0:T(8,128)}, f32[2,128,128]{2,1,0:T(8,128)}, f32[2,128,128]{2,1,0:T(8,128)}) custom-call(f32[512,256]{1,0:T(8,128)} %get-tuple-element.7.gx_ref, bf16[2,768,128]{2,1,0:T(8,128)(2,1)} %get-tuple-element.8.sum_ref), custom_call_target="tpu_custom_call" | custom-call | tf_op jit(solution)/shard_map/finish/pallas_call | solution.py:355

commit v3 on v2

--- a/solution.py
+++ b/solution.py
@@ -17,10 +17,9 @@
 
 
 def body(n, m, short_fast, x_ref, cot_ref, tiles_ref, mask_ref, wp_ref, wc_ref, ws_ref,
-         wn_ref, dil_ref, gx_ref, sum_ref, adj, x1, gat, th, sg, zt, acc, acc_t, uu, gx, cur,
+         wn_ref, dil_ref, gx_ref, sum_ref, adj, x1, gat, th, sg, zt, acc, acc_t, uu, gx, zb, cur,
          prv, gpre, halo, back, nxt, ag_r, ag_l, rs_out, rs_in, gp, r1, s2, fin, send, recv):
-    rows, wide = x_ref.shape
-    c = wide // 2
+    rows, c = x_ref.shape[1:]
     half = n // 2
     f = lax.axis_index("firm")
     t = lax.axis_index("tm")
@@ -113,16 +112,15 @@
 
     def current(l, x):
         for k in range(2):
-            cur[k] = dot(x[:, day(k)], wc_ref[l])
+            cur[k] = dot(x[k], wc_ref[l])
 
     def forward(l, x):
         d1 = dil_ref[l] == 1
-        h = halo[l].astype(F32)
-        h = h * jnp.where(t > 0, 1.0, 0.0)
+        some = jnp.where(t > 0, 1.0, 0.0)
         one = jnp.where(d1, 1.0, 0.0)
-        h0, h1 = h[:, day(0)], h[:, day(1)]
+        h0, h1 = halo[l, 0].astype(F32) * some, halo[l, 1].astype(F32) * some
         prv[l, :, day(0)] = (h1 * one + h0 * (1.0 - one)).astype(BF)
-        prv[l, :, day(1)] = (x[:, day(0)].astype(F32) * one + h1 * (1.0 - one)).astype(BF)
+        prv[l, :, day(1)] = (x[0].astype(F32) * one + h1 * (1.0 - one)).astype(BF)
         for k in range(2):
             pre = dot(prv[l, :, day(k)], wp_ref[l]) + cur[k]
             a = jnp.tanh(pre[:, :c])
@@ -132,36 +130,41 @@
             gat[l, :, day(k)] = (a * b).astype(BF)
 
     def pre_grad(l, zb, scatter):
+        cps = []
         for k in range(2):
-            gg = dot(zb[:, day(k)], ws_ref[l], 1, 1)
+            gg = dot(zb[k], ws_ref[l], 1, 1)
             scatter.end(k)
             gg = gg + dot(uu[:, day(k)], wn_ref[l], 1, 1)
             a, b = th[l, :, day(k)], sg[l, :, day(k)]
             gpre[k, :, :c] = (gg * b * (1.0 - a * a)).astype(BF)
             gpre[k, :, c:] = (gg * a * b * (1.0 - b)).astype(BF)
-            back[l, :, day(k)] = dot(gpre[k], wp_ref[l], 1, 1).astype(BF)
+            back[l, k] = dot(gpre[k], wp_ref[l], 1, 1).astype(BF)
+            cps.append(copy(back.at[l, k], nxt.at[l, k], tm=sooner))
+        return cps
 
     def direct(l, k):
         return dot(gpre[k], wc_ref[l], 1, 1)
 
     def shifted(l):
         one = jnp.where(dil_ref[l] == 1, 1.0, 0.0)
-        nb = nxt[l].astype(F32) * jnp.where(t < m - 1, 1.0, 0.0)
-        n0, n1 = nb[:, day(0)], nb[:, day(1)]
-        b1 = back[l, :, day(1)].astype(F32)
+        some = jnp.where(t < m - 1, 1.0, 0.0)
+        n0, n1 = nxt[l, 0].astype(F32) * some, nxt[l, 1].astype(F32) * some
+        b1 = back[l, 1].astype(F32)
         return (b1 * one + n0 * (1.0 - one), n0 * one + n1 * (1.0 - one))
+
+    def days(a):
+        return a[:, day(0)], a[:, day(1)]
 
     def weight_grads(l, x, zb, u):
         def total(a, b):
-            return dot(a[:, day(0)], b[0], 0, 0) + dot(a[:, day(1)], b[1], 0, 0)
+            return dot(a[0], b[0], 0, 0) + dot(a[1], b[1], 0, 0)
 
         pieces = []
         g2 = (gpre[0], gpre[1])
-        for w in (total(prv[l], g2), total(x, g2)):
+        for w in (total(days(prv[l]), g2), total(x, g2)):
             pieces += [w[:, :c], w[:, c:]]
-        z2 = (zb[:, day(0)], zb[:, day(1)])
-        u2 = (u[:, day(0)], u[:, day(1)])
-        pieces += [total(gat[l], z2), total(gat[l], u2)]
+        g = days(gat[l])
+        pieces += [total(g, zb), total(g, days(u))]
         gp[l] = jnp.concatenate(pieces, axis=0).astype(BF).reshape(gp.shape[1:])
 
     class Total:
@@ -197,67 +200,79 @@
                 cp.wait_recv()
             sum_ref[l] = fin[l].reshape(6 * c, c)
 
-    zt[1] = cot_ref[...].astype(F32).T.astype(BF)
+    for k in range(2):
+        zt[1, day(k)] = cot_ref[k].astype(F32).T.astype(BF)
     for q in (half, half - 1, 1 - half):
         build(pos + q)
     pl.semaphore_wait(barrier, n + m - 2)
     halo_cp = copy(x_ref, halo.at[0], tm=later)
     rs1 = Scatter(1)
     rs1.round(0)
-    x0 = x_ref[...]
-    current(0, x0)
+    current(0, x_ref)
     for q in range(2 - half, half - 1):
         build(pos + q)
     halo_cp.wait_recv()
-    forward(0, x0)
-
-    cps = [(copy(gat.at[0], ag_r.at[0], firm=right), copy(gat.at[0], ag_l.at[0], firm=left))]
+    forward(0, x_ref)
+
+    h = rows // 2
+    ring = ((ag_r, right), (ag_l, left))
+    cps = {}
+
+    def pass_on(dr, s, part):
+        rng = pl.ds(part * h, h)
+        buf, to = ring[dr]
+        src = buf.at[s - 1, rng] if s else gat.at[0, rng]
+        cps[dr, s, part] = copy(src, buf.at[s, rng], firm=to)
+
+    for dr in range(2):
+        pass_on(dr, 0, dr)
+    for dr in range(2):
+        pass_on(dr, 0, 1 - dr)
     acc[...] = dot(adj[:, block(pos)], gat[0])
     rs1.round(1)
-    for s in range(1, half + 1):
-        new = []
-        for dr, (buf, to) in enumerate(((ag_r, right), (ag_l, left))):
-            cps[s - 1][dr].wait_recv()
+    for s in range(1, half):
+        for dr in range(2):
+            cps[dr, s - 1, dr].wait_recv()
+            pass_on(dr, s, dr)
+        for dr in range(2):
+            cps[dr, s - 1, 1 - dr].wait_recv()
             if s < half - 1:
-                new.append(copy(buf.at[s - 1], buf.at[s], firm=to))
-            elif s == half - 1:
-                part = pl.ds(dr * (rows // 2), rows // 2)
-                new.append(copy(buf.at[s - 1, part], buf.at[s, part], firm=to))
-        cps.append(new)
-        if s < half:
-            acc[...] += (dot(adj[:, block(pos - s)], ag_r[s - 1])
-                         + dot(adj[:, block(pos + s)], ag_l[s - 1]))
-            if s < half - 2:
-                rs1.round(s + 1)
-            elif s == half - 1:
-                rs1.round(s)
-        else:
-            h = rows // 2
-            far = firm_at(pos + half) * rows
-            acc[...] += (dot(adj[:, pl.ds(pl.multiple_of(far, h), h)], ag_r[s - 1, :h])
-                         + dot(adj[:, pl.ds(pl.multiple_of(far + h, h), h)], ag_l[s - 1, h:]))
-    for k in range(2):
+                pass_on(dr, s, 1 - dr)
+        acc[...] += (dot(adj[:, block(pos - s)], ag_r[s - 1])
+                     + dot(adj[:, block(pos + s)], ag_l[s - 1]))
+        if 1 < s < half - 2:
+            rs1.round(s)
+        elif s == half - 1:
+            rs1.round(half - 2)
+    far = firm_at(pos + half) * rows
+    cps[0, half - 1, 0].wait_recv()
+    cps[1, half - 1, 1].wait_recv()
+    acc[...] += (dot(adj[:, pl.ds(pl.multiple_of(far, h), h)], ag_r[half - 1, :h])
+                 + dot(adj[:, pl.ds(pl.multiple_of(far + h, h), h)], ag_l[half - 1, h:]))
+    halo_cps = []
+    for k in (1, 0):
         mixed = (dot(gat[0, :, day(k)], ws_ref[0])
                  + dot(acc[:, day(k)].astype(BF), wn_ref[0]))
-        x1[:, day(k)] = (x_ref[:, day(k)].astype(F32) + mixed).astype(BF)
-    halo_cp = copy(x1, halo.at[1], tm=later)
-    current(1, x1[...])
+        x1[k] = (x_ref[k].astype(F32) + mixed).astype(BF)
+        halo_cps.append(copy(x1.at[k], halo.at[1, k], tm=later))
+    current(1, x1)
+    rs1.round(half - 1)
     rs1.own()
-    halo_cp.wait_recv()
-    forward(1, x1[...])
-
-    cot = cot_ref[...]
-    pre_grad(1, cot, rs1)
-    back_cp = copy(back.at[1], nxt.at[1], tm=sooner)
-    for k in range(2):
-        gx[:, day(k)] = cot[:, day(k)].astype(F32) + direct(1, k)
-    weight_grads(1, x1[...], cot, uu[...])
-    back_cp.wait_recv()
+    for cp in halo_cps:
+        cp.wait_recv()
+    forward(1, x1)
+
+    back_cps = pre_grad(1, cot_ref, rs1)
+    for k in range(2):
+        gx[k] = cot_ref[k].astype(F32) + direct(1, k)
+    weight_grads(1, x1, (cot_ref[0], cot_ref[1]), uu[...])
+    for cp in back_cps:
+        cp.wait_recv()
     sh = shifted(1)
     for k in range(2):
-        gx[:, day(k)] = gx[:, day(k)] + sh[k]
-    zb = gx[...].astype(BF)
-    zt[0] = gx[...].T.astype(BF)
+        gx[k] = gx[k] + sh[k]
+        zb[k] = gx[k].astype(BF)
+        zt[0, day(k)] = gx[k].T.astype(BF)
     rs0 = Scatter(0)
     rs0.round(0)
     sum1 = Total(1)
@@ -269,18 +284,18 @@
             sum1.second()
         if k == 2:
             sum1.third()
-    pre_grad(0, zb, rs0)
-    back_cp = copy(back.at[0], nxt.at[0], tm=sooner)
-    weight_grads(0, x0, zb, uu[...])
+    back_cps = pre_grad(0, zb, rs0)
+    weight_grads(0, x_ref, (zb[0], zb[1]), uu[...])
     sum0 = Total(0)
     sum0.first()
     for k in range(2):
-        gx[:, day(k)] = gx[:, day(k)] + direct(0, k)
+        gx[k] = gx[k] + direct(0, k)
+    for cp in back_cps:
+        cp.wait_recv()
+    sh = shifted(0)
+    for k in range(2):
+        gx_ref[k] = gx[k] + sh[k]
     sum0.second()
-    back_cp.wait_recv()
-    sh = shifted(0)
-    for k in range(2):
-        gx_ref[:, day(k)] = gx[:, day(k)] + sh[k]
     sum0.third()
     sum1.last()
     sum0.last()
@@ -291,7 +306,7 @@
 def finish(factor, gx_ref, sum_ref, out_ref, op_ref, oc_ref, os_ref, on_ref):
     c = on_ref.shape[-1]
     for k in range(2):
-        out_ref[:, k, :] = gx_ref[:, k * c:(k + 1) * c]
+        out_ref[:, k, :] = gx_ref[k]
     for l in range(L):
         g = sum_ref[l].astype(F32) * factor
         op_ref[l, :, :c] = g[:c]
@@ -308,20 +323,20 @@
     half = n // 2
     share = 6 * c // n
     factor = 1.0 / float(rows * n * days * m) ** 0.5
-    copies = 4 + 2 * half + 4 * (n - 1) + 2 * (2 * (n - 1) + m - 1)
+    copies = 7 + 6 * (n - 1) + 2 * (2 * (n - 1) + m - 1)
     vm = pl.BlockSpec(memory_space=pltpu.VMEM)
     sm = pl.BlockSpec(memory_space=pltpu.SMEM)
     flow, sums = pl.pallas_call(
         functools.partial(body, n, m, n == 8),
         out_shape=[
-            jax.ShapeDtypeStruct((rows, wide), F32),
+            jax.ShapeDtypeStruct((days, rows, c), F32),
             jax.ShapeDtypeStruct((L, 6 * c, c), BF),
         ],
         in_specs=[vm, vm, vm, sm, vm, vm, vm, vm, sm],
         out_specs=[vm] * 2,
         scratch_shapes=[
             pltpu.VMEM((rows, rows * n), BF),
-            pltpu.VMEM((rows, wide), BF),
+            pltpu.VMEM((days, rows, c), BF),
             pltpu.VMEM((L, rows, wide), BF),
             pltpu.VMEM((L, rows, wide), F32),
             pltpu.VMEM((L, rows, wide), F32),
@@ -329,13 +344,14 @@
             pltpu.VMEM((rows, wide), F32),
             pltpu.VMEM((wide, rows), F32),
             pltpu.VMEM((rows, wide), BF),
-            pltpu.VMEM((rows, wide), F32),
+            pltpu.VMEM((days, rows, c), F32),
+            pltpu.VMEM((days, rows, c), BF),
             pltpu.VMEM((2, rows, 2 * c), F32),
             pltpu.VMEM((L, rows, wide), BF),
             pltpu.VMEM((2, rows, 2 * c), BF),
-            pltpu.VMEM((L, rows, wide), BF),
-            pltpu.VMEM((L, rows, wide), BF),
-            pltpu.VMEM((L, rows, wide), BF),
+            pltpu.VMEM((L, days, rows, c), BF),
+            pltpu.VMEM((L, days, rows, c), BF),
+            pltpu.VMEM((L, days, rows, c), BF),
             pltpu.VMEM((half, rows, wide), BF),
             pltpu.VMEM((half, rows, wide), BF),
             pltpu.VMEM((L, 2, half, wide, rows), BF),
@@ -350,7 +366,7 @@
         compiler_params=pltpu.CompilerParams(
             collective_id=0, has_side_effects=True, vmem_limit_bytes=60 * 1024 * 1024),
         name="wavenet_backward",
-    )(features.reshape(rows, wide), cotangent.reshape(rows, wide), tiles, mask, w_prev, w_cur,
+    )(features.transpose(1, 0, 2), cotangent.transpose(1, 0, 2), tiles, mask, w_prev, w_cur,
       w_self, w_nbr, dilations)
     return pl.pallas_call(
         functools.partial(finish, factor),

time: 106 us -> 104 us (0.981)
  Pallas kernels: 103 us -> 101 us
    pallas_call x1, Pallas kernels: 101 us -> 98.9 us  [per_device(): pl.pallas_call(functools.partial(body, n, m, n == 8), out_shape=[jax.Shap...]
    reshape x1 -> x0, local copies, waits for them, and re-layouts: 1.89 us -> none  [per_device(): cotangent.reshape(rows, wide)]
    transpose x0 -> x1, local copies, waits for them, and re-layouts: none -> 1.89 us  [per_device(): cotangent.transpose(1, 0, 2)]
where the time goes in v3:
time: 104 us
  Pallas kernels  101 us (97%)
  local copies, waits for them, and re-layouts  1.89 us (2%)
    pallas_call x1, Pallas kernels, per_device(): pl.pallas_call(functools.partial(body, n, m, n == 8), out_shape=[jax.Shap...  98.9 us
    pallas_call x1, Pallas kernels, per_device(): pl.pallas_call(functools.partial(finish, factor), out_shape=[jax.ShapeDty...  2.39 us

profile of v3, /device:TPU:0, one launch (start us, length us, event | category | flops | bytes accessed | tf_op | source)
XLA Modules:
  0.0 103.8 jit_solution(16920175826256015219)
XLA Ops:
  0.6 1.9 %copy_bitcast_fusion = (bf16[2,512,128]{2,1,0:T(8,128)(2,1)}, bf16[2,512,128]{2,1,0:T(8,128)(2,1)}) fusion(bf16[512,2,128]{2,1,0:T(2,128)(2,1)} %param.10, bf16[512,2,128]{2,1,0:T(2,128)(2,1)} %param.9), kind=kLoop, calls=%fused_computation | loop fusion | bytes 1048576 | tf_op jit(solution)/shard_map/transpose | solution.py:369
  2.5 98.9 %wavenet_backward.1 = (f32[2,512,128]{2,1,0:T(8,128)}, bf16[2,768,128]{2,1,0:T(8,128)(2,1)}) custom-call(bf16[2,512,128]{2,1,0:T(8,128)(2,1)} %get-tuple-element.10.x_ref, bf16[2,512,128]{2,1,0:T(8,128)(2,1)} %get-tuple-element.9.cot_ref, bf16[4,32,128,128]{3,2,1,0:T(8,128)(2,1)} %tiles_ref.1, s32[4,32]{1,0:T(4,128)} %mask_ref.1, ...), custom_call_target="tpu_custom_call" | custom-call | tf_op jit(solution)/shard_map/wavenet_backward/pallas_call | solution.py:329
  101.4 2.4 %finish.1 = (f32[512,2,128]{2,1,0:T(2,128)}, f32[2,128,256]{2,1,0:T(8,128)}, f32[2,128,256]{2,1,0:T(8,128)}, f32[2,128,128]{2,1,0:T(8,128)}, f32[2,128,128]{2,1,0:T(8,128)}) custom-call(f32[2,512,128]{2,1,0:T(8,128)} %get-tuple-element.7.gx_ref, bf16[2,768,128]{2,1,0:T(8,128)(2,1)} %get-tuple-element.8.sum_ref), custom_call_target="tpu_custom_call" | custom-call | tf_op jit(solution)/shard_map/finish/pallas_call | solution.py:371

commit v4 on v3

--- a/solution.py
+++ b/solution.py
@@ -18,7 +18,7 @@
 
 def body(n, m, short_fast, x_ref, cot_ref, tiles_ref, mask_ref, wp_ref, wc_ref, ws_ref,
          wn_ref, dil_ref, gx_ref, sum_ref, adj, x1, gat, th, sg, zt, acc, acc_t, uu, gx, zb, cur,
-         prv, gpre, halo, back, nxt, ag_r, ag_l, rs_out, rs_in, gp, r1, s2, fin, send, recv):
+         prv, gpre, halo, back, nxt, ag_r, ag_l, rs_out, rs_in, gp, r0, p1, r1, fin, send, recv):
     rows, c = x_ref.shape[1:]
     half = n // 2
     f = lax.axis_index("firm")
@@ -165,6 +165,9 @@
             pieces += [w[:, :c], w[:, c:]]
         g = days(gat[l])
         pieces += [total(g, zb), total(g, days(u))]
+        spare = gp.shape[1] * gp.shape[2] * gp.shape[3] - 6 * c
+        if spare:
+            pieces.append(jnp.zeros((spare, c), F32))
         gp[l] = jnp.concatenate(pieces, axis=0).astype(BF).reshape(gp.shape[1:])
 
     class Total:
@@ -172,33 +175,41 @@
             self.l = l
 
         def first(self):
-            self.a = [copy(gp.at[self.l, (f + o) % n], r1.at[self.l, o - 1], firm=(f + o) % n)
-                      for o in range(1, n)]
+            l = self.l
+            self.a = [copy(gp.at[l, (t + o) % m], r0.at[l, o - 1], tm=(t + o) % m)
+                      for o in range(1, m)]
 
         def second(self):
             l = self.l
-            s = gp[l, f].astype(F32)
-            for o in range(1, n):
+            s = gp[l, t].astype(F32)
+            for o in range(1, m):
                 self.a[o - 1].wait_recv()
-                s = s + r1[l, o - 1].astype(F32)
-            s2[l, t] = s.astype(BF)
-            self.b = [copy(s2.at[l, t], s2.at[l, t], tm=(t + o) % m) for o in range(1, m)]
+                s = s + r0[l, o - 1].astype(F32)
+            p1[l] = s.astype(BF)
+            self.b = [copy(p1.at[l, (f + o) % n], r1.at[l, o - 1], firm=(f + o) % n)
+                      for o in range(1, n)]
 
         def third(self):
             l = self.l
-            for cp in self.b:
-                cp.wait_recv()
-            s = s2[l, 0].astype(F32)
-            for j in range(1, m):
-                s = s + s2[l, j].astype(F32)
-            fin[l, f] = s.astype(BF)
-            self.d = [copy(fin.at[l, f], fin.at[l, f], firm=(f + o) % n) for o in range(1, n)]
-
-        def last(self):
+            s = p1[l, f].astype(F32)
+            for o in range(1, n):
+                self.b[o - 1].wait_recv()
+                s = s + r1[l, o - 1].astype(F32)
+            fin[l, t, f] = s.astype(BF)
+            self.d = [copy(fin.at[l, t, f], fin.at[l, t, f], firm=(f + o) % n)
+                      for o in range(1, n)]
+
+        def fourth(self):
             l = self.l
             for cp in self.d:
                 cp.wait_recv()
-            sum_ref[l] = fin[l].reshape(6 * c, c)
+            self.e = [copy(fin.at[l, t], fin.at[l, t], tm=(t + o) % m) for o in range(1, m)]
+
+        def last(self):
+            l = self.l
+            for cp in self.e:
+                cp.wait_recv()
+            sum_ref[l] = fin[l].reshape(-1, c)[:6 * c]
 
     for k in range(2):
         zt[1, day(k)] = cot_ref[k].astype(F32).T.astype(BF)
@@ -284,6 +295,8 @@
             sum1.second()
         if k == 2:
             sum1.third()
+        if k == half - 1:
+            sum1.fourth()
     back_cps = pre_grad(0, zb, rs0)
     weight_grads(0, x_ref, (zb[0], zb[1]), uu[...])
     sum0 = Total(0)
@@ -298,6 +311,7 @@
     sum0.second()
     sum0.third()
     sum1.last()
+    sum0.fourth()
     sum0.last()
     for cp in started:
         cp.wait_send()
@@ -321,9 +335,9 @@
     rows, days, c = features.shape
     wide = days * c
     half = n // 2
-    share = 6 * c // n
+    share = -(-6 * c // (n * m * 16)) * 16
     factor = 1.0 / float(rows * n * days * m) ** 0.5
-    copies = 7 + 6 * (n - 1) + 2 * (2 * (n - 1) + m - 1)
+    copies = 7 + 6 * (n - 1) + 4 * (n - 1 + m - 1)
     vm = pl.BlockSpec(memory_space=pltpu.VMEM)
     sm = pl.BlockSpec(memory_space=pltpu.SMEM)
     flow, sums = pl.pallas_call(
@@ -356,10 +370,11 @@
             pltpu.VMEM((half, rows, wide), BF),
             pltpu.VMEM((L, 2, half, wide, rows), BF),
             pltpu.VMEM((L, 2, half, wide, rows), BF),
+            pltpu.VMEM((L, m, n, share, c), BF),
+            pltpu.VMEM((L, m - 1, n, share, c), BF),
             pltpu.VMEM((L, n, share, c), BF),
             pltpu.VMEM((L, n - 1, share, c), BF),
-            pltpu.VMEM((L, m, share, c), BF),
-            pltpu.VMEM((L, n, share, c), BF),
+            pltpu.VMEM((L, m, n, share, c), BF),
             pltpu.SemaphoreType.DMA((copies,)),
             pltpu.SemaphoreType.DMA((copies,)),
         ],

time: 104 us -> 103 us (level)
  no operation moved by 1% of the time
where the time goes in v4:
time: 103 us
  Pallas kernels  101 us (98%)
  local copies, waits for them, and re-layouts  1.89 us (2%)
    pallas_call x1, Pallas kernels, per_device(): pl.pallas_call(functools.partial(body, n, m, n == 8), out_shape=[jax.Shap...  98.3 us
    pallas_call x1, Pallas kernels, per_device(): pl.pallas_call(functools.partial(finish, factor), out_shape=[jax.ShapeDty...  2.39 us

profile of v4, /device:TPU:0, one launch (start us, length us, event | category | flops | bytes accessed | tf_op | source)
XLA Modules:
  0.0 103.3 jit_solution(13115653744347647670)
XLA Ops:
  0.6 1.9 %copy_bitcast_fusion = (bf16[2,512,128]{2,1,0:T(8,128)(2,1)}, bf16[2,512,128]{2,1,0:T(8,128)(2,1)}) fusion(bf16[512,2,128]{2,1,0:T(2,128)(2,1)} %param.10, bf16[512,2,128]{2,1,0:T(2,128)(2,1)} %param.9), kind=kLoop, calls=%fused_computation | loop fusion | bytes 1048576 | tf_op jit(solution)/shard_map/transpose | solution.py:384
  2.5 98.3 %wavenet_backward.1 = (f32[2,512,128]{2,1,0:T(8,128)}, bf16[2,768,128]{2,1,0:T(8,128)(2,1)}) custom-call(bf16[2,512,128]{2,1,0:T(8,128)(2,1)} %get-tuple-element.10.x_ref, bf16[2,512,128]{2,1,0:T(8,128)(2,1)} %get-tuple-element.9.cot_ref, bf16[4,32,128,128]{3,2,1,0:T(8,128)(2,1)} %tiles_ref.1, s32[4,32]{1,0:T(4,128)} %mask_ref.1, ...), custom_call_target="tpu_custom_call" | custom-call | tf_op jit(solution)/shard_map/wavenet_backward/pallas_call | solution.py:343
  100.9 2.4 %finish.1 = (f32[512,2,128]{2,1,0:T(2,128)}, f32[2,128,256]{2,1,0:T(8,128)}, f32[2,128,256]{2,1,0:T(8,128)}, f32[2,128,128]{2,1,0:T(8,128)}, f32[2,128,128]{2,1,0:T(8,128)}) custom-call(f32[2,512,128]{2,1,0:T(8,128)} %get-tuple-element.7.gx_ref, bf16[2,768,128]{2,1,0:T(8,128)(2,1)} %get-tuple-element.8.sum_ref), custom_call_target="tpu_custom_call" | custom-call | tf_op jit(solution)/shard_map/finish/pallas_call | solution.py:386

commit v5 on v4

--- a/solution.py
+++ b/solution.py
@@ -276,7 +276,6 @@
     back_cps = pre_grad(1, cot_ref, rs1)
     for k in range(2):
         gx[k] = cot_ref[k].astype(F32) + direct(1, k)
-    weight_grads(1, x1, (cot_ref[0], cot_ref[1]), uu[...])
     for cp in back_cps:
         cp.wait_recv()
     sh = shifted(1)
@@ -286,6 +285,7 @@
         zt[0, day(k)] = gx[k].T.astype(BF)
     rs0 = Scatter(0)
     rs0.round(0)
+    weight_grads(1, x1, (cot_ref[0], cot_ref[1]), uu[...])
     sum1 = Total(1)
     sum1.first()
     rs0.own()

time: 103 us -> 103 us (level)
  no operation moved by 1% of the time
where the time goes in v5:
time: 103 us
  Pallas kernels  100 us (97%)
  local copies, waits for them, and re-layouts  1.89 us (2%)
    pallas_call x1, Pallas kernels, per_device(): pl.pallas_call(functools.partial(body, n, m, n == 8), out_shape=[jax.Shap...  97.9 us
    pallas_call x1, Pallas kernels, per_device(): pl.pallas_call(functools.partial(finish, factor), out_shape=[jax.ShapeDty...  2.39 us

profile of v5, /device:TPU:0, one launch (start us, length us, event | category | flops | bytes accessed | tf_op | source)
XLA Modules:
  0.0 102.9 jit_solution(13913810431398626744)
XLA Ops:
  0.6 1.9 %copy_bitcast_fusion = (bf16[2,512,128]{2,1,0:T(8,128)(2,1)}, bf16[2,512,128]{2,1,0:T(8,128)(2,1)}) fusion(bf16[512,2,128]{2,1,0:T(2,128)(2,1)} %param.10, bf16[512,2,128]{2,1,0:T(2,128)(2,1)} %param.9), kind=kLoop, calls=%fused_computation | loop fusion | bytes 1048576 | tf_op jit(solution)/shard_map/transpose | solution.py:384
  2.5 97.9 %wavenet_backward.1 = (f32[2,512,128]{2,1,0:T(8,128)}, bf16[2,768,128]{2,1,0:T(8,128)(2,1)}) custom-call(bf16[2,512,128]{2,1,0:T(8,128)(2,1)} %get-tuple-element.10.x_ref, bf16[2,512,128]{2,1,0:T(8,128)(2,1)} %get-tuple-element.9.cot_ref, bf16[4,32,128,128]{3,2,1,0:T(8,128)(2,1)} %tiles_ref.1, s32[4,32]{1,0:T(4,128)} %mask_ref.1, ...), custom_call_target="tpu_custom_call" | custom-call | tf_op jit(solution)/shard_map/wavenet_backward/pallas_call | solution.py:343
  100.5 2.4 %finish.1 = (f32[512,2,128]{2,1,0:T(2,128)}, f32[2,128,256]{2,1,0:T(8,128)}, f32[2,128,256]{2,1,0:T(8,128)}, f32[2,128,128]{2,1,0:T(8,128)}, f32[2,128,128]{2,1,0:T(8,128)}) custom-call(f32[2,512,128]{2,1,0:T(8,128)} %get-tuple-element.7.gx_ref, bf16[2,768,128]{2,1,0:T(8,128)(2,1)} %get-tuple-element.8.sum_ref), custom_call_target="tpu_custom_call" | custom-call | tf_op jit(solution)/shard_map/finish/pallas_call | solution.py:386
